TPU v7x, 32 devices: a whole 2x2x4 slice. The times are simulated.
32 devices in a mesh: dp: 8 (over z, y), rep: 4 (over x, core).
Axes of the slice: x: 2, y: 2, z: 4, core: 2. Of those that a mesh axis runs over, the one named last changes fastest.
Arguments:
- clip_input: bfloat16 [32, 4, 20, 20, 832], P(('dp', 'rep')), may hold values from -6 to 6
- cotangent: bfloat16 [32, 2, 10, 10, 832], P(('dp', 'rep')), may hold values from -6 to 6
- clip_group: int32 [32], P(('dp', 'rep')), may hold values from 0 to 2
- crop_sides: int32 [3], replicated, may hold values from 14 to 20, as said below
- w_single: bfloat16 [2, 832, 256], replicated, may hold values from -0.21875 to 0.21875
- w_reduce: bfloat16 [2, 832, 160], replicated, may hold values from -0.21875 to 0.21875
- w_spatial: bfloat16 [2, 3, 3, 3, 160, 320], replicated, may hold values from -0.09375 to 0.09375
- w_squeeze: bfloat16 [2, 832, 32], replicated, may hold values from -0.21875 to 0.21875
- w_narrow: bfloat16 [2, 3, 3, 3, 32, 128], replicated, may hold values from -0.21875 to 0.21875
- w_project: bfloat16 [2, 832, 128], replicated, may hold values from -0.21875 to 0.21875
- bn_scale: float32 [2, 1024], replicated, may hold values from 0.1 to 1.9
- bn_shift: float32 [2, 1024], replicated, may hold values from -3 to 3
Outputs:
- activations: bfloat16 [32, 2, 10, 10, 832], P(('dp', 'rep'))
- input_grad: bfloat16 [32, 4, 20, 20, 832], P(('dp', 'rep'))
- grad_single: float32 [2, 832, 256], replicated
- grad_reduce: float32 [2, 832, 160], replicated
- grad_spatial: float32 [2, 3, 3, 3, 160, 320], replicated
- grad_squeeze: float32 [2, 832, 32], replicated
- grad_narrow: float32 [2, 3, 3, 3, 32, 128], replicated
- grad_project: float32 [2, 832, 128], replicated
- grad_scale: float32 [2, 1024], replicated
- grad_shift: float32 [2, 1024], replicated
Inputs may be any that keep to these rules, and one draw needn't show every extreme that they name: `crop_sides`: the three entries are 20, 16 and 14, in an order drawn from the seed.
All inputs are finite; a program needn't handle non-finite values.
Results may differ from a plain program's by a relative error of at most 0.015.
Values sent between devices are 32-bit elements; how exact they have to be, the bound alone decides.
No kernel may reach another device: no remote copies, remote signals or barrier semaphores. Data moves between devices by JAX's collectives and lax.ppermute only.
A program may use at most 320 MiB of HBM per device.

v0:
```python
import jax
import jax.numpy as jnp
from jax import lax
from jax.sharding import PartitionSpec as P


def mask_for(sides, frames, side):
    place = jnp.arange(side, dtype=jnp.int32)
    inside = (place[None, :, None] < sides[:, None, None]) & (
        place[None, None, :] < sides[:, None, None]
    )
    return jnp.broadcast_to(
        inside[:, None, :, :, None], (sides.shape[0], frames, side, side, 1)
    ).astype(jnp.float32)


def crop_masks(clip_group, crop_sides, frames, side):
    choose = (clip_group[:, None] == jnp.arange(3, dtype=jnp.int32)[None, :]).astype(jnp.int32)
    sides = jnp.sum(choose * crop_sides[None, :], axis=1)
    return (mask_for(sides, frames, side), mask_for(sides // 2, frames // 2, side // 2))


def neighbour_mean(value):
    for axis in (1, 2, 3):
        pads = [(0, 0)] * 5
        pads[axis] = (1, 1)
        padded = jnp.pad(value, pads)
        length = value.shape[axis]
        value = (
            lax.slice_in_dim(padded, 0, length, axis=axis)
            + lax.slice_in_dim(padded, 1, length + 1, axis=axis)
            + lax.slice_in_dim(padded, 2, length + 2, axis=axis)
        )
    return value / 27.0


def pool_pairs(value):
    n, t, h, w, c = value.shape
    return jnp.mean(value.reshape(n, t // 2, 2, h // 2, 2, w // 2, 2, c), axis=(2, 4, 6))


def spread_pairs(grad):
    n, t, h, w, c = grad.shape
    wide = jnp.broadcast_to(grad[:, :, None, :, None, :, None, :], (n, t, 2, h, 2, w, 2, c))
    return wide.reshape(n, 2 * t, 2 * h, 2 * w, c) / 8.0


def point_forward(value, kernel):
    return jnp.einsum("nthwc,cd->nthwd", value, kernel, preferred_element_type=jnp.float32)


def point_backward(value, kernel, grad_low):
    kernel_grad = jnp.einsum("nthwc,nthwd->cd", value, grad_low, preferred_element_type=jnp.float32)
    value_grad = jnp.einsum("nthwd,cd->nthwc", grad_low, kernel, preferred_element_type=jnp.float32)
    return (kernel_grad, value_grad)


def spatial_forward(value, kernel):
    n, t, h, w, c = value.shape
    padded = jnp.pad(value, ((0, 0), (1, 1), (1, 1), (1, 1), (0, 0)))
    total = jnp.zeros((n, t, h, w, kernel.shape[-1]), jnp.float32)
    for first in range(3):
        for second in range(3):
            for third in range(3):
                window = padded[:, first : first + t, second : second + h, third : third + w]
                total = total + jnp.einsum(
                    "nthwc,cd->nthwd",
                    window,
                    kernel[first, second, third],
                    preferred_element_type=jnp.float32,
                )
    return total


def spatial_backward(value, kernel, grad_low):
    n, t, h, w, c = value.shape
    padded = jnp.pad(value, ((0, 0), (1, 1), (1, 1), (1, 1), (0, 0)))
    padded_grad = jnp.pad(grad_low, ((0, 0), (1, 1), (1, 1), (1, 1), (0, 0)))
    taps = []
    value_grad = jnp.zeros((n, t, h, w, c), jnp.float32)
    for first in range(3):
        for second in range(3):
            for third in range(3):
                window = padded[:, first : first + t, second : second + h, third : third + w]
                taps.append(
                    jnp.einsum(
                        "nthwc,nthwd->cd", window, grad_low, preferred_element_type=jnp.float32
                    )
                )
                back = padded_grad[
                    :,
                    2 - first : 2 - first + t,
                    2 - second : 2 - second + h,
                    2 - third : 2 - third + w,
                ]
                value_grad = value_grad + jnp.einsum(
                    "nthwd,cd->nthwc",
                    back,
                    kernel[first, second, third],
                    preferred_element_type=jnp.float32,
                )
    kernel_grad = jnp.stack(taps).reshape(3, 3, 3, c, grad_low.shape[-1])
    return (kernel_grad, value_grad)


def local_stats(pre, mask):
    return jnp.stack(
        [jnp.sum(pre * mask, axis=(0, 1, 2, 3)), jnp.sum(pre * pre * mask, axis=(0, 1, 2, 3))]
    )


def sync_stats(parts):
    return [lax.psum(item, ("dp", "rep")) for item in parts]


def normalize(pre, sums, count, gamma, beta, mask):
    mean = sums[0] / count
    square = sums[1] / count
    inverse = lax.rsqrt(square - mean * mean + 1e-05)
    normed = (pre - mean) * inverse
    shifted = gamma * normed + beta
    return (jax.nn.silu(shifted) * mask, (normed, shifted, inverse))


def unit_terms(grad_out, kept, mask):
    normed, shifted, inverse = kept
    gate_value = jax.nn.sigmoid(shifted)
    grad_shift = grad_out * mask * (gate_value * (1.0 + shifted * (1.0 - gate_value)))
    sums = jnp.stack(
        [jnp.sum(grad_shift, axis=(0, 1, 2, 3)), jnp.sum(grad_shift * normed, axis=(0, 1, 2, 3))]
    )
    return (grad_shift, sums)


def unit_grad(grad_shift, kept, gamma, sums, count, mask):
    normed, shifted, inverse = kept
    full = gamma * inverse * (grad_shift - sums[0] / count - normed * (sums[1] / count)) * mask
    return full.astype(jnp.bfloat16)


def split_params(kernels, vector):
    w_single, w_reduce, w_spatial, w_squeeze, w_narrow, w_project = kernels
    widths = [
        w_single.shape[1],
        w_reduce.shape[1],
        w_spatial.shape[-1],
        w_squeeze.shape[1],
        w_narrow.shape[-1],
        w_project.shape[1],
    ]
    pieces = []
    start = 0
    for width in widths:
        pieces.append(vector[start : start + width])
        start = start + width
    return pieces


def block_forward(source, kernels, gains, offsets, mask, count):
    w_single, w_reduce, w_spatial, w_squeeze, w_narrow, w_project = kernels
    gamma = split_params(kernels, gains)
    beta = split_params(kernels, offsets)
    z_single = point_forward(source, w_single)
    z_reduce = point_forward(source, w_reduce)
    z_squeeze = point_forward(source, w_squeeze)
    pooled_low = neighbour_mean(source.astype(jnp.float32)).astype(jnp.bfloat16)
    z_project = point_forward(pooled_low, w_project)
    first = sync_stats(
        [local_stats(item, mask) for item in (z_single, z_reduce, z_squeeze, z_project)]
    )
    out_single, keep_single = normalize(z_single, first[0], count, gamma[0], beta[0], mask)
    out_reduce, keep_reduce = normalize(z_reduce, first[1], count, gamma[1], beta[1], mask)
    out_squeeze, keep_squeeze = normalize(z_squeeze, first[2], count, gamma[3], beta[3], mask)
    out_project, keep_project = normalize(z_project, first[3], count, gamma[5], beta[5], mask)
    reduce_low = out_reduce.astype(jnp.bfloat16)
    squeeze_low = out_squeeze.astype(jnp.bfloat16)
    z_spatial = spatial_forward(reduce_low, w_spatial)
    z_narrow = spatial_forward(squeeze_low, w_narrow)
    second = sync_stats([local_stats(z_spatial, mask), local_stats(z_narrow, mask)])
    out_spatial, keep_spatial = normalize(z_spatial, second[0], count, gamma[2], beta[2], mask)
    out_narrow, keep_narrow = normalize(z_narrow, second[1], count, gamma[4], beta[4], mask)
    result = jnp.concatenate([out_single, out_spatial, out_narrow, out_project], axis=-1)
    inputs = (source, reduce_low, squeeze_low, pooled_low)
    kept = (keep_single, keep_reduce, keep_spatial, keep_squeeze, keep_narrow, keep_project)
    return (result, (inputs, kept))


def block_backward(grad_out, saved, kernels, gains, mask, count):
    w_single, w_reduce, w_spatial, w_squeeze, w_narrow, w_project = kernels
    inputs, kept = saved
    source, reduce_low, squeeze_low, pooled_low = inputs
    keep_single, keep_reduce, keep_spatial, keep_squeeze, keep_narrow, keep_project = kept
    gamma = split_params(kernels, gains)
    edge_one = w_single.shape[1]
    edge_two = edge_one + w_spatial.shape[-1]
    edge_three = edge_two + w_narrow.shape[-1]
    grad_single = grad_out[..., :edge_one]
    grad_spatial = grad_out[..., edge_one:edge_two]
    grad_narrow = grad_out[..., edge_two:edge_three]
    grad_project = grad_out[..., edge_three:]
    shift_spatial, sums_spatial = unit_terms(grad_spatial, keep_spatial, mask)
    shift_narrow, sums_narrow = unit_terms(grad_narrow, keep_narrow, mask)
    second = sync_stats([sums_spatial, sums_narrow])
    dz_spatial = unit_grad(shift_spatial, keep_spatial, gamma[2], second[0], count, mask)
    dz_narrow = unit_grad(shift_narrow, keep_narrow, gamma[4], second[1], count, mask)
    kernel_spatial, grad_reduce = spatial_backward(reduce_low, w_spatial, dz_spatial)
    kernel_narrow, grad_squeeze = spatial_backward(squeeze_low, w_narrow, dz_narrow)
    shift_single, sums_single = unit_terms(grad_single, keep_single, mask)
    shift_reduce, sums_reduce = unit_terms(grad_reduce, keep_reduce, mask)
    shift_squeeze, sums_squeeze = unit_terms(grad_squeeze, keep_squeeze, mask)
    shift_project, sums_project = unit_terms(grad_project, keep_project, mask)
    first = sync_stats([sums_single, sums_reduce, sums_squeeze, sums_project])
    dz_single = unit_grad(shift_single, keep_single, gamma[0], first[0], count, mask)
    dz_reduce = unit_grad(shift_reduce, keep_reduce, gamma[1], first[1], count, mask)
    dz_squeeze = unit_grad(shift_squeeze, keep_squeeze, gamma[3], first[2], count, mask)
    dz_project = unit_grad(shift_project, keep_project, gamma[5], first[3], count, mask)
    kernel_single, from_single = point_backward(source, w_single, dz_single)
    kernel_reduce, from_reduce = point_backward(source, w_reduce, dz_reduce)
    kernel_squeeze, from_squeeze = point_backward(source, w_squeeze, dz_squeeze)
    kernel_project, from_pooled = point_backward(pooled_low, w_project, dz_project)
    source_grad = from_single + from_reduce + from_squeeze + neighbour_mean(from_pooled)
    order = [first[0], first[1], second[0], first[2], second[1], first[3]]
    scale_grad = jnp.concatenate([item[1] for item in order])
    shift_grad = jnp.concatenate([item[0] for item in order])
    kernel_grads = (
        kernel_single,
        kernel_reduce,
        kernel_spatial,
        kernel_squeeze,
        kernel_narrow,
        kernel_project,
    )
    return (source_grad, kernel_grads, scale_grad, shift_grad)


def shards(
    clip_input,
    cotangent,
    clip_group,
    crop_sides,
    w_single,
    w_reduce,
    w_spatial,
    w_squeeze,
    w_narrow,
    w_project,
    bn_scale,
    bn_shift,
):
    mask, small_mask = crop_masks(clip_group, crop_sides, clip_input.shape[1], clip_input.shape[2])
    count = lax.psum(jnp.sum(mask), ("dp", "rep"))
    small_count = count / 8.0
    lower = (w_single[0], w_reduce[0], w_spatial[0], w_squeeze[0], w_narrow[0], w_project[0])
    upper = (w_single[1], w_reduce[1], w_spatial[1], w_squeeze[1], w_narrow[1], w_project[1])
    source = clip_input * mask.astype(jnp.bfloat16)
    first_out, first_saved = block_forward(source, lower, bn_scale[0], bn_shift[0], mask, count)
    middle = pool_pairs(first_out).astype(jnp.bfloat16)
    second_out, second_saved = block_forward(
        middle, upper, bn_scale[1], bn_shift[1], small_mask, small_count
    )
    middle_grad, upper_grads, upper_scale, upper_shift = block_backward(
        cotangent.astype(jnp.float32), second_saved, upper, bn_scale[1], small_mask, small_count
    )
    source_grad, lower_grads, lower_scale, lower_shift = block_backward(
        spread_pairs(middle_grad), first_saved, lower, bn_scale[0], mask, count
    )
    joined = [
        jnp.stack([low_item, high_item]) for low_item, high_item in zip(lower_grads, upper_grads)
    ]
    stacked = lax.psum(
        (joined[0], joined[1], joined[2], joined[3], joined[4], joined[5]), ("dp", "rep")
    )
    input_grad = (source_grad * mask).astype(jnp.bfloat16)
    return (
        second_out.astype(jnp.bfloat16),
        input_grad,
        stacked[0],
        stacked[1],
        stacked[2],
        stacked[3],
        stacked[4],
        stacked[5],
        jnp.stack([lower_scale, upper_scale]),
        jnp.stack([lower_shift, upper_shift]),
    )


def solution(mesh):
    placed = (
        P(("dp", "rep"), None, None, None, None),
        P(("dp", "rep"), None, None, None, None),
        P(("dp", "rep")),
        P(),
        P(),
        P(),
        P(),
        P(),
        P(),
        P(),
        P(),
        P(),
    )
    return jax.shard_map(
        shards,
        mesh=mesh,
        in_specs=placed,
        out_specs=(
            P(("dp", "rep"), None, None, None, None),
            P(("dp", "rep"), None, None, None, None),
            P(),
            P(),
            P(),
            P(),
            P(),
            P(),
            P(),
            P(),
        ),
        check_vma=False,
    )
```

profile of v0, /device:TPU:0, one launch (start us, length us, event | category | flops | bytes accessed | tf_op | source)
XLA Modules:
  0.0 1140.0 jit_solution(2134734077063902635)
XLA Ops:
  10.5 3.4 multiply_reduce_fusion.4
  16.3 3.4 slice_bitcast_fusion
  19.7 42.4 %all-reduce.27 = (f32[2,32]{1,0:T(2,128)S(1)}, f32[]{:T(128)}, f32[2,160]{1,0:T(2,128)S(1)}) all-reduce(f32[2,32]{1,0:T(2,128)S(1)} %pad_maximum_fusion.21, f32[]{:T(128)} %broadcast_reduce_fusion, f32[2,160]{1,0:T(2,128)S(1)} %pad_maximum_fusion.14), channel_id=1, replica_groups=mesh['dp'=8,'rep'=4] {'dp','rep'}, use_global_device_ids=true, to_apply=%region_14.15 | all-reduce | flops 385 | bytes 3080 | tf_op jit(solution)/shard_map/psum | solution.py:113
  63.9 3.4 fusion.591
  69.6 2.4 fusion.593
  83.4 2.4 fusion.599
  90.3 2.4 fusion.602
  104.0 2.8 fusion.610
  109.0 2.3 fusion.612
  122.7 2.9 fusion.605
  129.7 5.1 fusion.19
  140.9 26.9 %multiply_reduce_fusion.1 = (f32[320]{0:T(512)S(1)}, f32[320]{0:T(512)S(1)}, f32[4,20,20,320]{3,2,1,0:T(8,128)}) fusion(f32[20,20]{1,0:T(8,128)S(1)} %get-tuple-element.366, bf16[3,3,3,160,320]{4,3,2,1,0:T(8,128)(2,1)} %get-tuple-element.174, bf16[1,4,20,20,160]{4,3,2,1,0:T(8,128)(2,1)S(1)} %fusion.1140, f32[4,20,20,320]{3,2,1,0:T(8,128)} %fusion.617, ...), kind=kOutput, calls=%fused_computation.119 | convolution fusion | flops 179711360 | bytes 79364160 | tf_op jit(solution)/shard_map/nthwc,cd->nthwd/dot_general | solution.py:66
  182.1 2.5 fusion.10
  184.7 3.0 multiply_reduce_fusion.6
  189.8 40.8 %all-reduce.26 = (f32[2,128]{1,0:T(2,128)S(1)}, f32[2,128]{1,0:T(2,128)S(1)}, f32[2,320]{1,0:T(2,128)S(1)}, f32[2,256]{1,0:T(2,128)S(1)}) all-reduce(f32[2,128]{1,0:T(2,128)S(1)} %pad_maximum_fusion.23, f32[2,128]{1,0:T(2,128)S(1)} %pad_maximum_fusion.22, ...), channel_id=1, replica_groups=mesh['dp'=8,'rep'=4] {'dp','rep'}, use_global_device_ids=true, to_apply=%region_20.21 | all-reduce | flops 1664 | bytes 13312 | tf_op jit(solution)/shard_map/psum | solution.py:113
  231.9 3.5 multiply_multiply_fusion.2
  235.3 3.1 reshape.3177
  238.5 4.1 copy.1227
  243.9 2.6 multiply_multiply_fusion
  246.4 4.4 reshape.3178
  250.9 3.0 copy.1228
  257.3 8.9 maximum_reduce_fusion
  271.1 39.8 %all-reduce.25 = (f32[2,32]{1,0:T(2,128)S(1)}, f32[2,160]{1,0:T(2,128)S(1)}) all-reduce(f32[2,32]{1,0:T(2,128)S(1)} %pad_maximum_fusion.24, f32[2,160]{1,0:T(2,128)S(1)} %pad_maximum_fusion.16), channel_id=1, replica_groups=mesh['dp'=8,'rep'=4] {'dp','rep'}, use_global_device_ids=true, to_apply=%region_33.34 | all-reduce | flops 384 | bytes 3072 | tf_op jit(solution)/shard_map/psum | solution.py:113
  329.6 40.5 %all-reduce.24 = (f32[2,128]{1,0:T(2,128)}, f32[2,320]{1,0:T(2,128)}) all-reduce(f32[2,128]{1,0:T(2,128)} %pad_maximum_fusion.25, f32[2,320]{1,0:T(2,128)S(1)} %pad_maximum_fusion.10), channel_id=1, replica_groups=mesh['dp'=8,'rep'=4] {'dp','rep'}, use_global_device_ids=true, to_apply=%region_36.37 | all-reduce | flops 896 | bytes 7168 | tf_op jit(solution)/shard_map/psum | solution.py:113
  381.0 40.6 %all-reduce.23 = (f32[2,128]{1,0:T(2,128)}, f32[2,256]{1,0:T(2,128)}, f32[2,320]{1,0:T(2,128)}, f32[2,128]{1,0:T(2,128)}) all-reduce(f32[2,128]{1,0:T(2,128)} %pad_maximum_fusion.26, f32[2,256]{1,0:T(2,128)} %pad_maximum_fusion.15, f32[2,320]{1,0:T(2,128)} %pad_maximum_fusion.11, ...), channel_id=1, replica_groups=mesh['dp'=8,'rep'=4] {'dp','rep'}, use_global_device_ids=true, to_apply=%region_39.40 | all-reduce | flops 1664 | bytes 13312 | tf_op jit(solution)/shard_map/psum | solution.py:113
  447.2 41.4 %all-reduce.22 = (f32[2,256]{1,0:T(2,128)}, f32[2,160]{1,0:T(2,128)}, f32[2,32]{1,0:T(2,128)}, f32[2,128]{1,0:T(2,128)}) all-reduce(f32[2,256]{1,0:T(2,128)} %pad_maximum_fusion.17, f32[2,160]{1,0:T(2,128)} %pad_maximum_fusion.18, f32[2,32]{1,0:T(2,128)} %pad_maximum_fusion.28, ...), channel_id=1, replica_groups=mesh['dp'=8,'rep'=4] {'dp','rep'}, use_global_device_ids=true, to_apply=%region_42.43 | all-reduce | flops 1152 | bytes 9216 | tf_op jit(solution)/shard_map/psum | solution.py:113
  496.7 4.0 broadcast_in_dim.5
  500.7 8.5 div.814
  509.2 3.8 fusion.1112
  516.0 3.0 fusion.1091
  519.0 40.2 %all-reduce.21 = (f32[2,320]{1,0:T(2,128)S(1)}, f32[2,128]{1,0:T(2,128)S(1)}) all-reduce(f32[2,320]{1,0:T(2,128)S(1)} %pad_maximum_fusion.12, f32[2,128]{1,0:T(2,128)S(1)} %pad_maximum_fusion.30), channel_id=1, replica_groups=mesh['dp'=8,'rep'=4] {'dp','rep'}, use_global_device_ids=true, to_apply=%region_63.64 | all-reduce | flops 896 | bytes 7168 | tf_op jit(solution)/shard_map/psum | solution.py:113
  559.9 3.7 fusion.16
  595.2 2.4 fusion.77
  617.5 5.7 fusion.341
  625.3 3.3 fusion.272
  628.6 8.0 fusion.273
  660.6 2.5 fusion.1093
  663.1 19.4 %fusion.1092 = (f32[160]{0:T(256)S(1)}, f32[160]{0:T(256)S(1)}, f32[4,20,20,160]{3,2,1,0:T(8,128)}) fusion(f32[160]{0:T(256)S(1)} %copy-done.247, f32[4,20,20,160]{3,2,1,0:T(8,128)} %copy-done.10, f32[160]{0:T(256)S(1)} %bitcast.3314, f32[160]{0:T(256)S(1)} %bitcast.3344, f32[160]{0:T(256)S(1)} %bitcast.3324, f32[20,20]{1,0:T(8,128)S(1)} %get-tuple-element.366, ...), kind=kOutput, calls=%fused_computation.1726 | convolution fusion | flops 174591680 | bytes 55260480 | tf_op jit(solution)/shard_map/nthwd,cd->nthwc/dot_general | solution.py:96
  682.6 40.4 %all-reduce.20 = (f32[2,128]{1,0:T(2,128)}, f32[2,256]{1,0:T(2,128)S(1)}, f32[2,160]{1,0:T(2,128)S(1)}, f32[2,32]{1,0:T(2,128)}) all-reduce(f32[2,128]{1,0:T(2,128)S(1)} %pad_maximum_fusion.32, f32[2,256]{1,0:T(2,128)S(1)} %pad_maximum_fusion.19, f32[2,160]{1,0:T(2,128)S(1)} %pad_maximum_fusion.20, ...), channel_id=1, replica_groups=mesh['dp'=8,'rep'=4] {'dp','rep'}, use_global_device_ids=true, to_apply=%region_75.76 | all-reduce | flops 1152 | bytes 9216 | tf_op jit(solution)/shard_map/psum | solution.py:113
  798.9 2.7 copy-done.24
  801.6 10.8 pad_maximum_fusion
  820.4 4.8 fusion.432
  826.3 3.6 fusion.3
  829.9 13.0 %fusion.9 = bf16[1,4,20,20,832]{4,3,2,1,0:T(8,128)(2,1)} fusion(f32[1,4,20,20,832]{4,3,2,1,0:T(8,128)} %fusion.3, f32[4,20,20,832]{3,2,1,0:T(8,128)} %fusion.432, f32[4,20,20,832]{3,2,1,0:T(8,128)S(1)} %fusion.449, f32[20,20]{1,0:T(8,128)S(1)} %get-tuple-element.366, bf16[4,20,20,32]{3,2,1,0:T(8,128)(2,1)S(1)} %copy-done.54, ...), kind=kOutput, calls=%fused_computation.45 | convolution fusion | flops 95846400 | bytes 20754432 | tf_op jit(solution)/shard_map/nthwd,cd->nthwc/dot_general | solution.py:54
  843.0 5.4 copy.994
  852.1 263.7 %all-reduce.31.cloned.1.call-done = (f32[2,832,256]{2,1,0:T(8,128)}, f32[2,832,160]{1,2,0:T(8,128)}, f32[2,3,3,3,160,320]{5,4,3,2,1,0:T(8,128)}, f32[2,832,32]{1...) async-done(((f32[2,832,256]{2,1,0:T(8,128)}, f32[2,832,160]{1,2,0:T(8,128)}, f32[2,3,3,3,160,320]{5,4,3,2,1,0:T(8,128)}, f32[2,832,32]{1,2,0:T(8,128)}, ...) | async-done | bytes 15777808 | tf_op jit(solution)/shard_map/psum | solution.py:270
  1115.8 2.8 copy.1851
  1119.6 10.7 copy.1853
  (1245 shorter events, 316.1 us)
Async XLA Ops:
  7.2 1108.6 %all-reduce.31.cloned.1.call-start = ((), (), s32[]{:S(2)}) async-start(), calls=%async_computation | async-start | bytes 36175872 | tf_op jit(solution)/shard_map/psum | solution.py:270
  13.9 108.8 %copy-start.10 = (f32[4,20,20,160]{3,2,1,0:T(8,128)}, f32[4,20,20,160]{3,2,1,0:T(8,128)S(1)}, u32[]{:S(2)}) copy-start(f32[4,20,20,160]{3,2,1,0:T(8,128)S(1)} %get-tuple-element.369) | copy-start | bytes 3072004
  16.2 106.5 %copy-start.235 = (f32[1,160]{1,0:T(1,128)}, f32[1,160]{1,0:T(1,128)S(1)}, u32[]{:S(2)}) copy-start(f32[1,160]{1,0:T(1,128)S(1)} %get-tuple-element.304) | copy-start | bytes 1924
  16.2 301.5 %copy-start.262 = (f32[1,160]{1,0:T(1,128)}, f32[1,160]{1,0:T(1,128)S(1)}, u32[]{:S(2)}) copy-start(f32[1,160]{1,0:T(1,128)S(1)} %get-tuple-element.303) | copy-start | bytes 1924
  16.3 106.4 %copy-start.259 = (f32[1,160]{1,0:T(1,128)}, f32[1,160]{1,0:T(1,128)S(1)}, u32[]{:S(2)}) copy-start(f32[1,160]{1,0:T(1,128)S(1)} %get-tuple-element.306) | copy-start | bytes 1924
  16.3 301.5 %copy-start.334 = (f32[1,160]{1,0:T(1,128)}, f32[1,160]{1,0:T(1,128)S(1)}, u32[]{:S(2)}) copy-start(f32[1,160]{1,0:T(1,128)S(1)} %get-tuple-element.305) | copy-start | bytes 1924
  62.7 60.0 %copy-start.219 = (f32[1,160]{1,0:T(1,128)}, f32[1,160]{1,0:T(1,128)S(1)}, u32[]{:S(2)}) copy-start(f32[1,160]{1,0:T(1,128)S(1)} %get-tuple-element.340) | copy-start | bytes 1924
  63.2 59.5 %copy-start.246 = (f32[160]{0:T(256)}, f32[160]{0:T(256)S(1)}, u32[]{:S(2)}) copy-start(f32[160]{0:T(256)S(1)} %get-tuple-element.319) | copy-start | bytes 1924
  126.2 8.5 copy-start.306
  126.8 7.9 copy-start.308
  128.1 6.7 copy-start.285
  128.1 6.6 copy-start.299
  135.3 96.6 %copy-start.249 = (f32[1,256]{1,0:T(1,128)}, f32[1,256]{1,0:T(1,128)S(1)}, u32[]{:S(2)}) copy-start(f32[1,256]{1,0:T(1,128)S(1)} %get-tuple-element.290) | copy-start | bytes 3076
  135.8 96.0 %copy-start.283 = (f32[1,256]{1,0:T(1,128)}, f32[1,256]{1,0:T(1,128)S(1)}, u32[]{:S(2)}) copy-start(f32[1,256]{1,0:T(1,128)S(1)} %get-tuple-element.292) | copy-start | bytes 3076
  137.1 106.7 %copy-start.224 = (f32[320]{0:T(512)}, f32[320]{0:T(512)S(1)}, u32[]{:S(2)}) copy-start(f32[320]{0:T(512)S(1)} %get-tuple-element.103) | copy-start | bytes 3844
  137.7 117.4 %copy-start.324 = (f32[128]{0:T(128)}, f32[128]{0:T(128)S(1)}, u32[]{:S(2)}) copy-start(f32[128]{0:T(128)S(1)} %get-tuple-element.297) | copy-start | bytes 1540
  137.7 117.4 %copy-start.328 = (f32[128]{0:T(128)}, f32[128]{0:T(128)S(1)}, u32[]{:S(2)}) copy-start(f32[128]{0:T(128)S(1)} %get-tuple-element.298) | copy-start | bytes 1540
  138.3 116.8 %copy-start.326 = (f32[128]{0:T(128)}, f32[128]{0:T(128)S(1)}, u32[]{:S(2)}) copy-start(f32[128]{0:T(128)S(1)} %get-tuple-element.300) | copy-start | bytes 1540
  138.3 116.8 %copy-start.330 = (f32[128]{0:T(128)}, f32[128]{0:T(128)S(1)}, u32[]{:S(2)}) copy-start(f32[128]{0:T(128)S(1)} %get-tuple-element.301) | copy-start | bytes 1540
  140.9 26.9 %copy-start.141 = (bf16[2,3,3,3,32,128]{5,4,3,2,1,0:T(8,128)(2,1)S(1)}, bf16[2,3,3,3,32,128]{5,4,3,2,1,0:T(8,128)(2,1)}, u32[]{:S(2)}) copy-start(bf16[2,3,3,3,32,128]{5,4,3,2,1,0:T(8,128)(2,1)} %param.20) | copy-start | bytes 1327108
  168.6 20.4 %copy-start.56 = (bf16[3,3,3,32,128]{4,3,2,1,0:T(8,128)(2,1)}, bf16[3,3,3,32,128]{4,3,2,1,0:T(8,128)(2,1)S(1)}, u32[]{:S(2)}) copy-start(bf16[3,3,3,32,128]{4,3,2,1,0:T(8,128)(2,1)S(1)} %get-tuple-element.231) | copy-start | bytes 663556
  189.0 66.2 %copy-start.6 = (f32[4,20,20,128]{3,2,1,0:T(8,128)}, f32[4,20,20,128]{3,2,1,0:T(8,128)S(1)}, u32[]{:S(2)}) copy-start(f32[4,20,20,128]{3,2,1,0:T(8,128)S(1)} %fusion.515) | copy-start | bytes 2457604
  189.8 323.3 %copy-start.12 = (f32[4,20,20,128]{3,2,1,0:T(8,128)}, f32[4,20,20,128]{3,2,1,0:T(8,128)S(1)}, u32[]{:S(2)}) copy-start(f32[4,20,20,128]{3,2,1,0:T(8,128)S(1)} %get-tuple-element.370) | copy-start | bytes 2457604
  231.3 7.2 copy-start.221
  267.4 44.2 %copy-start.26 = (bf16[2,10,10,832]{3,2,1,0:T(8,128)(2,1)}, bf16[2,10,10,832]{3,2,1,0:T(8,128)(2,1)S(1)}, u32[]{:S(2)}) copy-start(bf16[2,10,10,832]{3,2,1,0:T(8,128)(2,1)S(1)} %get-tuple-element.172) | copy-start | bytes 998404
  267.8 43.8 %copy-start.70 = (f32[2,10,10,160]{3,2,1,0:T(8,128)}, f32[2,10,10,160]{3,2,1,0:T(8,128)S(1)}, u32[]{:S(2)}) copy-start(f32[2,10,10,160]{3,2,1,0:T(8,128)S(1)} %get-tuple-element.374) | copy-start | bytes 384004
  310.9 6.9 copy-start.237
  321.4 112.1 %copy-start.20 = (f32[2,10,10,320]{3,2,1,0:T(8,128)}, f32[2,10,10,320]{3,2,1,0:T(8,128)S(1)}, u32[]{:S(2)}) copy-start(f32[2,10,10,320]{3,2,1,0:T(8,128)S(1)} %get-tuple-element.376) | copy-start | bytes 768004
  328.3 97.4 %copy-start.32 = (f32[2,10,10,128]{3,2,1,0:T(8,128)}, f32[2,10,10,128]{3,2,1,0:T(8,128)S(1)}, u32[]{:S(2)}) copy-start(f32[2,10,10,128]{3,2,1,0:T(8,128)S(1)} %fusion.518) | copy-start | bytes 307204
  329.0 94.6 %copy-start.46 = (f32[2,10,10,128]{3,2,1,0:T(8,128)}, f32[2,10,10,128]{3,2,1,0:T(8,128)S(1)}, u32[]{:S(2)}) copy-start(f32[2,10,10,128]{3,2,1,0:T(8,128)S(1)} %get-tuple-element.375) | copy-start | bytes 307204
  370.2 10.2 copy-start.361
  370.2 10.2 copy-start.362
  373.4 60.1 %copy-start.209 = (f32[320]{0:T(512)}, f32[320]{0:T(512)S(1)}, u32[]{:S(2)}) copy-start(f32[320]{0:T(512)S(1)} %get-tuple-element.110) | copy-start | bytes 3844
  421.6 7.4 copy-start.59
  440.5 48.9 %copy-start.33 = (f32[2,10,10,128]{3,2,1,0:T(8,128)S(1)}, f32[2,10,10,128]{3,2,1,0:T(8,128)}, u32[]{:S(2)}) copy-start(f32[2,10,10,128]{3,2,1,0:T(8,128)} %copy-done.32) | copy-start | bytes 307204
  441.9 51.7 %copy-start.217 = (f32[1,256]{1,0:T(1,128)}, f32[1,256]{1,0:T(1,128)S(1)}, u32[]{:S(2)}) copy-start(f32[1,256]{1,0:T(1,128)S(1)} %get-tuple-element.334) | copy-start | bytes 3076
  559.1 85.0 %copy-start.341 = (f32[2,128]{1,0:T(2,128)}, f32[2,128]{1,0:T(2,128)S(1)}, u32[]{:S(2)}) copy-start(f32[2,128]{1,0:T(2,128)S(1)} %get-tuple-element.119) | copy-start | bytes 3076
  723.0 42.1 %copy-start.273 = (f32[1,256]{1,0:T(1,128)}, f32[1,256]{1,0:T(1,128)S(1)}, u32[]{:S(2)}) copy-start(f32[1,256]{1,0:T(1,128)S(1)} %get-tuple-element.325) | copy-start | bytes 3076
  723.0 42.7 %copy-start.277 = (f32[1,256]{1,0:T(1,128)}, f32[1,256]{1,0:T(1,128)S(1)}, u32[]{:S(2)}) copy-start(f32[1,256]{1,0:T(1,128)S(1)} %get-tuple-element.324) | copy-start | bytes 3076
  723.0 36.3 %copy-start.275 = (f32[1,160]{1,0:T(1,128)}, f32[1,160]{1,0:T(1,128)S(1)}, u32[]{:S(2)}) copy-start(f32[1,160]{1,0:T(1,128)S(1)} %get-tuple-element.321) | copy-start | bytes 1924
  723.0 37.0 %copy-start.279 = (f32[1,160]{1,0:T(1,128)}, f32[1,160]{1,0:T(1,128)S(1)}, u32[]{:S(2)}) copy-start(f32[1,160]{1,0:T(1,128)S(1)} %get-tuple-element.320) | copy-start | bytes 1924
  801.6 10.8 copy-start.181
  801.6 10.8 copy-start.182
  801.6 11.5 %copy-start.142 = (f32[1,832,128]{2,1,0:T(8,128)S(1)}, f32[1,832,128]{2,1,0:T(8,128)}, u32[]{:S(2)}) copy-start(f32[1,832,128]{2,1,0:T(8,128)} %convolution_bitcast_fusion.4) | copy-start | bytes 1277956
  801.6 11.5 %copy-start.143 = (f32[1,832,128]{2,1,0:T(8,128)S(1)}, f32[1,832,128]{2,1,0:T(8,128)}, u32[]{:S(2)}) copy-start(f32[1,832,128]{2,1,0:T(8,128)} %fusion.120) | copy-start | bytes 1277956
  801.6 12.5 %copy-start.116 = (f32[1,832,160]{1,2,0:T(8,128)S(1)}, f32[1,832,160]{1,2,0:T(8,128)}, u32[]{:S(2)}) copy-start(f32[1,832,160]{1,2,0:T(8,128)} %fusion.117) | copy-start | bytes 1597444
  1119.6 10.7 copy-start.153
  1119.6 11.4 %copy-start.103 = (f32[2,3,3,3,32,128]{5,4,3,2,1,0:T(8,128)S(1)}, f32[2,3,3,3,32,128]{5,4,3,2,1,0:T(8,128)}, u32[]{:S(2)}) copy-start(f32[2,3,3,3,32,128]{5,4,3,2,1,0:T(8,128)} %get-tuple-element.390) | copy-start | bytes 2654212
  (327 other events, 729.8 us)
Sparse Core Ops, SparseCore 0:
  816.7 299.0 all-reduce.30
where the time goes:
time: 1150 us; the launch traced here: 1140 us
  blocking collectives  326 us (28%)
  matrix products  299 us (26%)
  waiting for transfers between devices  264 us (23%)
  local copies, waits for them, and re-layouts  123 us (11%)
  other arithmetic  104 us (9%)
  between operations  24 us (2%)
    psum x8, blocking collectives, sync_stats(): return [lax.psum(item, ('dp', 'rep')) for item in parts]  326 us
    psum x1, waiting for transfers between devices, shards(): lax.psum((joined[0], joined[1], joined[2], joined[3], joined[4], joined[5...  264 us
    dot_general x108, matrix products, spatial_forward(): jnp.einsum('nthwc,cd->nthwd', window, kernel[first, second, third], prefe...  114 us
    dot_general x108, matrix products, spatial_backward(): jnp.einsum('nthwd,cd->nthwc', back, kernel[first, second, third], preferr...  99.8 us
    unnamed x752, local copies, waits for them, and re-layouts  56.8 us
    dot_general x108, matrix products, spatial_backward(): jnp.einsum('nthwc,nthwd->cd', window, grad_low, preferred_element_type=jn...  37.9 us
    another operation x8, local copies, waits for them, and re-layouts  24 us
  transfers between devices with their start and end apart: 1, of which 1 were waited for; matrix products, arithmetic and copies ran while one was open for 3% of the time, Pallas kernels for 0%

commit v1 on v0

--- a/solution.py
+++ b/solution.py
@@ -55,51 +55,32 @@
     return (kernel_grad, value_grad)
 
 
+CONV_FORM = ("NDHWC", "DHWIO", "NDHWC")
+CONV_PADS = [(1, 1), (1, 1), (1, 1)]
+
+
 def spatial_forward(value, kernel):
-    n, t, h, w, c = value.shape
-    padded = jnp.pad(value, ((0, 0), (1, 1), (1, 1), (1, 1), (0, 0)))
-    total = jnp.zeros((n, t, h, w, kernel.shape[-1]), jnp.float32)
-    for first in range(3):
-        for second in range(3):
-            for third in range(3):
-                window = padded[:, first : first + t, second : second + h, third : third + w]
-                total = total + jnp.einsum(
-                    "nthwc,cd->nthwd",
-                    window,
-                    kernel[first, second, third],
-                    preferred_element_type=jnp.float32,
-                )
-    return total
+    return lax.conv_general_dilated(
+        value,
+        kernel,
+        (1, 1, 1),
+        CONV_PADS,
+        dimension_numbers=CONV_FORM,
+        preferred_element_type=jnp.float32,
+    )
 
 
 def spatial_backward(value, kernel, grad_low):
-    n, t, h, w, c = value.shape
-    padded = jnp.pad(value, ((0, 0), (1, 1), (1, 1), (1, 1), (0, 0)))
-    padded_grad = jnp.pad(grad_low, ((0, 0), (1, 1), (1, 1), (1, 1), (0, 0)))
-    taps = []
-    value_grad = jnp.zeros((n, t, h, w, c), jnp.float32)
-    for first in range(3):
-        for second in range(3):
-            for third in range(3):
-                window = padded[:, first : first + t, second : second + h, third : third + w]
-                taps.append(
-                    jnp.einsum(
-                        "nthwc,nthwd->cd", window, grad_low, preferred_element_type=jnp.float32
-                    )
-                )
-                back = padded_grad[
-                    :,
-                    2 - first : 2 - first + t,
-                    2 - second : 2 - second + h,
-                    2 - third : 2 - third + w,
-                ]
-                value_grad = value_grad + jnp.einsum(
-                    "nthwd,cd->nthwc",
-                    back,
-                    kernel[first, second, third],
-                    preferred_element_type=jnp.float32,
-                )
-    kernel_grad = jnp.stack(taps).reshape(3, 3, 3, c, grad_low.shape[-1])
+    turned = jnp.swapaxes(jnp.flip(kernel, (0, 1, 2)), 3, 4)
+    value_grad = spatial_forward(grad_low, turned)
+    kernel_grad = lax.conv_general_dilated(
+        value,
+        grad_low,
+        (1, 1, 1),
+        CONV_PADS,
+        dimension_numbers=("CDHWN", "IDHWO", "DHWNC"),
+        preferred_element_type=jnp.float32,
+    )
     return (kernel_grad, value_grad)
 
 

time: 1150 us -> 1030 us (0.90)
  matrix products: 299 us -> 165 us
  other arithmetic: 104 us -> 136 us
  local copies, waits for them, and re-layouts: 123 us -> 108 us
    dot_general x324 -> x0, matrix products: 251 us -> none  [the longest x108 114 us: spatial_forward(): jnp.einsum('nthwc,cd->nthwd', window, kernel[first, second, third], prefe...]
    conv_general_dilated x0 -> x12, matrix products: none -> 118 us  [the longest x4 70 us: spatial_backward(): lax.conv_general_dilated(value, grad_low, (1, 1, 1), CONV_PADS, dimension...]
    psum x0 -> x1, blocking collectives: none -> 42.6 us  [shards(): count = lax.psum(jnp.sum(mask), ('dp', 'rep'))]
    psum x8 -> x7, blocking collectives: 326 us -> 284 us  [sync_stats(): return [lax.psum(item, ('dp', 'rep')) for item in parts]]
    another operation x8 -> x0, local copies, waits for them, and re-layouts: 24 us -> none
    unnamed x752 -> x521, local copies, waits for them, and re-layouts: 56.8 us -> 40.6 us
    mul x0 -> x11, local copies, waits for them, and re-layouts: none -> 12.9 us  [the longest x3 5.22 us: normalize(): normed = (pre - mean) * inverse]
where the time goes in v1:
time: 1030 us; the launch traced here: 1020 us
  blocking collectives  326 us (32%)
  waiting for transfers between devices  265 us (26%)
  matrix products  165 us (16%)
  other arithmetic  136 us (13%)
  local copies, waits for them, and re-layouts  108 us (10%)
  between operations  21.8 us (2%)
    psum x7, blocking collectives, sync_stats(): return [lax.psum(item, ('dp', 'rep')) for item in parts]  284 us
    psum x1, waiting for transfers between devices, shards(): lax.psum((joined[0], joined[1], joined[2], joined[3], joined[4], joined[5...  265 us
    conv_general_dilated x4, matrix products, spatial_backward(): lax.conv_general_dilated(value, grad_low, (1, 1, 1), CONV_PADS, dimension...  70 us
    conv_general_dilated x8, matrix products, spatial_forward(): lax.conv_general_dilated(value, kernel, (1, 1, 1), CONV_PADS, dimension_n...  47.5 us
    psum x1, blocking collectives, shards(): count = lax.psum(jnp.sum(mask), ('dp', 'rep'))  42.6 us
    unnamed x521, local copies, waits for them, and re-layouts  40.6 us
    dot_general x8, matrix products, point_backward(): jnp.einsum('nthwd,cd->nthwc', grad_low, kernel, preferred_element_type=jn...  21.9 us
    reduce_sum x12, other arithmetic, unit_terms(): jnp.sum(grad_shift, axis=(0, 1, 2, 3))  20.6 us
  transfers between devices with their start and end apart: 1, of which 1 were waited for; matrix products, arithmetic and copies ran while one was open for 3% of the time, Pallas kernels for 0%

profile of v1, /device:TPU:0, one launch (start us, length us, event | category | flops | bytes accessed | tf_op | source)
XLA Modules:
  0.0 1022.4 jit_solution(5501252164632307690)
XLA Ops:
  25.3 4.7 fusion.29
  35.1 3.8 fusion.11
  39.5 42.6 %all-reduce.19 = (f32[]{:T(128)}, f32[2,32]{1,0:T(2,128)S(1)}, f32[2,160]{1,0:T(2,128)S(1)}) all-reduce(f32[]{:T(128)} %broadcast_reduce_fusion, f32[2,32]{1,0:T(2,128)S(1)} %pad_maximum_fusion.21, f32[2,160]{1,0:T(2,128)S(1)} %pad_maximum_fusion.14), channel_id=1, replica_groups=mesh['dp'=8,'rep'=4] {'dp','rep'}, use_global_device_ids=true, to_apply=%region_5.6 | all-reduce | flops 385 | bytes 3080 | tf_op jit(solution)/shard_map/psum | solution.py:232
  91.3 9.8 fusion.344
  101.1 1.9 copy.167
  103.0 1.9 copy.168
  106.9 3.1 multiply_reduce_fusion.3
  111.9 40.5 %all-reduce.18 = (f32[2,128]{1,0:T(2,128)S(1)}, f32[2,128]{1,0:T(2,128)S(1)}, f32[2,320]{1,0:T(2,128)S(1)}, f32[2,256]{1,0:T(2,128)S(1)}) all-reduce(f32[2,128]{1,0:T(2,128)S(1)} %pad_maximum_fusion.23, f32[2,128]{1,0:T(2,128)S(1)} %pad_maximum_fusion.22, ...), channel_id=1, replica_groups=mesh['dp'=8,'rep'=4] {'dp','rep'}, use_global_device_ids=true, to_apply=%region_20.21 | all-reduce | flops 1664 | bytes 13312 | tf_op jit(solution)/shard_map/psum | solution.py:94
  162.2 2.8 add_multiply_fusion
  168.7 4.0 copy.170
  173.9 1.9 multiply_multiply_fusion
  175.8 3.8 reshape.1442
  179.6 17.9 %maximum_reduce_fusion = f32[2,10,10,832]{3,2,1,0:T(8,128)S(1)} fusion(f32[1,2,2,10,2,10,2,128]{7,0,6,5,4,3,2,1:T(1,128)} %copy.180, f32[1,2,2,10,2,10,2,128]{7,0,6,5,4,3,2,1:T(1,128)} %copy.179, f32[1,2,2,10,2,10,2,320]{7,0,6,5,4,3,2,1:T(1,128)} %bitcast.719, f32[1,2,2,10,2,10,2,256]{7,0,6,5,4,3,2,1:T(1,128)} %reshape.1442), kind=kLoop, calls=%fused_computation.21 | loop fusion | flops 5158400 | bytes 5990400 | tf_op jit(solution)/shard_map/reduce_sum | solution.py:39
  203.6 3.6 copy.199
  214.6 40.2 %all-reduce.17 = (f32[2,32]{1,0:T(2,128)}, f32[2,160]{1,0:T(2,128)}) all-reduce(f32[2,32]{1,0:T(2,128)} %pad_maximum_fusion.24, f32[2,160]{1,0:T(2,128)S(1)} %pad_maximum_fusion.16), channel_id=1, replica_groups=mesh['dp'=8,'rep'=4] {'dp','rep'}, use_global_device_ids=true, to_apply=%region_33.34 | all-reduce | flops 384 | bytes 3072 | tf_op jit(solution)/shard_map/psum | solution.py:94
  257.8 2.2 fusion.213
  263.9 6.4 fusion.16
  271.6 40.9 %all-reduce.16 = (f32[2,128]{1,0:T(2,128)}, f32[2,320]{1,0:T(2,128)}) all-reduce(f32[2,128]{1,0:T(2,128)} %pad_maximum_fusion.25, f32[2,320]{1,0:T(2,128)S(1)} %pad_maximum_fusion.10), channel_id=1, replica_groups=mesh['dp'=8,'rep'=4] {'dp','rep'}, use_global_device_ids=true, to_apply=%region_36.37 | all-reduce | flops 896 | bytes 7168 | tf_op jit(solution)/shard_map/psum | solution.py:94
  315.6 2.2 fusion.317
  324.1 40.5 %all-reduce.15 = (f32[2,128]{1,0:T(2,128)}, f32[2,256]{1,0:T(2,128)}, f32[2,320]{1,0:T(2,128)}, f32[2,128]{1,0:T(2,128)}) all-reduce(f32[2,128]{1,0:T(2,128)} %pad_maximum_fusion.26, f32[2,256]{1,0:T(2,128)} %pad_maximum_fusion.15, f32[2,320]{1,0:T(2,128)} %pad_maximum_fusion.11, ...), channel_id=1, replica_groups=mesh['dp'=8,'rep'=4] {'dp','rep'}, use_global_device_ids=true, to_apply=%region_39.40 | all-reduce | flops 1664 | bytes 13312 | tf_op jit(solution)/shard_map/psum | solution.py:94
  369.4 10.9 %fusion.14 = f32[1,2,10,10,160]{4,0,3,2,1:T(1,128)S(1)} fusion(bf16[2,3,3,3,160,320]{5,4,3,2,1,0:T(8,128)(2,1)} %param.18, bf16[1,2,10,10,320]{4,3,2,1,0:T(8,128)(2,1)S(1)} %fusion.156), kind=kOutput, calls=%fused_computation.28 | convolution fusion | flops 321126400 | bytes 3573760 | tf_op jit(solution)/shard_map/conv_general_dilated | solution.py:63
  385.9 1.9 fusion.319
  390.1 41.0 %all-reduce.14 = (f32[2,256]{1,0:T(2,128)}, f32[2,160]{1,0:T(2,128)}, f32[2,32]{1,0:T(2,128)}, f32[2,128]{1,0:T(2,128)}) all-reduce(f32[2,256]{1,0:T(2,128)} %pad_maximum_fusion.17, f32[2,160]{1,0:T(2,128)} %pad_maximum_fusion.18, f32[2,32]{1,0:T(2,128)} %pad_maximum_fusion.28, ...), channel_id=1, replica_groups=mesh['dp'=8,'rep'=4] {'dp','rep'}, use_global_device_ids=true, to_apply=%region_42.43 | all-reduce | flops 1152 | bytes 9216 | tf_op jit(solution)/shard_map/psum | solution.py:94
  440.7 4.0 broadcast_in_dim.5
  444.7 8.8 div.810
  453.6 3.7 fusion.334
  461.0 8.0 convolution_bitcast_fusion.2
  471.7 2.1 convolution_bitcast_fusion.6
  478.1 2.7 fusion.312
  482.5 39.8 %all-reduce.13 = (f32[2,320]{1,0:T(2,128)S(1)}, f32[2,128]{1,0:T(2,128)S(1)}) all-reduce(f32[2,320]{1,0:T(2,128)S(1)} %pad_maximum_fusion.12, f32[2,128]{1,0:T(2,128)S(1)} %pad_maximum_fusion.30), channel_id=1, replica_groups=mesh['dp'=8,'rep'=4] {'dp','rep'}, use_global_device_ids=true, to_apply=%region_63.64 | all-reduce | flops 896 | bytes 7168 | tf_op jit(solution)/shard_map/psum | solution.py:94
  526.3 2.5 fusion.314
  535.3 11.8 %fusion.75 = f32[4,20,8,3,160]{4,2,3,1,0:T(8,128)S(1)} fusion(bf16[2,3,3,3,160,320]{5,4,3,2,1,0:T(8,128)(2,1)S(1)} %bitcast.842, bf16[4,20,1,7,2,320]{5,3,4,1,0,2:T(8,128)(2,1)S(1)} %slice.623, bf16[4,20,1,8,3,320]{5,3,4,1,0,2:T(8,128)(2,1)S(1)} %copy.202, pred[8,3]{0,1:T(4,128)(4,1)S(1)} %copy-done.248), kind=kOutput, calls=%fused_computation.125 | convolution fusion | flops 4282675200 | bytes 7004672 | tf_op jit(solution)/shard_map/conv_general_dilated | solution.py:63
  550.4 2.6 fusion.313
  556.0 3.8 convolution_select_fusion
  562.7 40.8 %all-reduce.12 = (f32[2,128]{1,0:T(2,128)S(1)}, f32[2,256]{1,0:T(2,128)S(1)}, f32[2,160]{1,0:T(2,128)S(1)}, f32[2,32]{1,0:T(2,128)S(1)}) all-reduce(f32[2,128]{1,0:T(2,128)S(1)} %pad_maximum_fusion.32, f32[2,256]{1,0:T(2,128)S(1)} %pad_maximum_fusion.19, ...), channel_id=1, replica_groups=mesh['dp'=8,'rep'=4] {'dp','rep'}, use_global_device_ids=true, to_apply=%region_75.76 | all-reduce | flops 1152 | bytes 9216 | tf_op jit(solution)/shard_map/psum | solution.py:94
  608.5 2.8 fusion.105
  611.7 2.1 fusion.84
  616.1 49.8 %convolution_bitcast_fusion.1 = f32[1,3,3,3,160,320]{5,4,3,2,1,0:T(8,128)} fusion(bf16[1,4,20,20,320]{4,1,3,2,0:T(4,128)(2,1)} %copy-done.28, bf16[1,4,20,20,160]{4,3,2,1,0:T(8,128)(2,1)} %fusion.359), kind=kOutput, calls=%fused_computation.50 | convolution fusion | flops 3444736000 | bytes 7065600 | tf_op jit(solution)/shard_map/conv_general_dilated | solution.py:76
  667.7 2.7 fusion.102
  670.5 10.0 convolution_bitcast_fusion.7
  685.2 11.0 %pad_maximum_fusion = f32[2,3,3,3,160,320]{5,4,3,2,1,0:T(8,128)} fusion(f32[1,3,3,3,160,320]{5,4,3,2,1,0:T(8,128)} %convolution_bitcast_fusion.2, f32[1,3,3,3,160,320]{5,4,3,2,1,0:T(8,128)} %convolution_bitcast_fusion.1), kind=kLoop, calls=%fused_computation | loop fusion | flops 2764800 | bytes 22118400 | tf_op jit(solution)/shard_map/stack | solution.py:249
  704.1 4.1 fusion.168
  709.0 3.6 fusion.3
  712.7 12.9 %fusion.9 = bf16[1,4,20,20,832]{4,3,2,1,0:T(8,128)(2,1)} fusion(f32[1,4,20,20,832]{4,3,2,1,0:T(8,128)} %fusion.3, f32[4,20,20,832]{3,2,1,0:T(8,128)} %fusion.168, f32[4,20,20,832]{3,2,1,0:T(8,128)S(1)} %fusion.191, f32[20,20]{1,0:T(8,128)S(1)} %copy-done.25, bf16[4,20,20,32]{3,2,1,0:T(8,128)(2,1)S(1)} %fusion.160, bf16[2,832,32]{1,2,0:T(8,128)(2,1)S(1)} %copy-done.104), kind=kOutput, calls=%fused_computation.19 | convolution fusion | flops 95846400 | bytes 20754432 | tf_op jit(solution)/shard_map/nthwd,cd->nthwc/dot_general | solution.py:54
  725.7 5.1 copy.243
  732.6 265.4 %all-reduce.23.cloned.1.call-done = (f32[2,832,256]{2,1,0:T(8,128)}, f32[2,832,160]{1,2,0:T(8,128)}, f32[2,3,3,3,160,320]{5,4,3,2,1,0:T(8,128)}, f32[2,832,32]{1...) async-done(((f32[2,832,256]{2,1,0:T(8,128)}, f32[2,832,160]{1,2,0:T(8,128)}, f32[2,3,3,3,160,320]{5,4,3,2,1,0:T(8,128)}, f32[2,832,32]{1,2,0:T(8,128)}, ...) | async-done | bytes 15777808 | tf_op jit(solution)/shard_map/psum | solution.py:251
  998.0 2.8 copy.487
  1001.8 10.7 %copy.489 = f32[2,3,3,3,160,320]{5,4,3,2,1,0:T(8,128)} copy(f32[2,3,3,3,160,320]{5,4,3,2,1,0:T(8,128)} %get-tuple-element.269) | data formatting | bytes 22118400
  (735 shorter events, 158.4 us)
Async XLA Ops:
  7.2 990.8 %all-reduce.23.cloned.1.call-start = ((), (), s32[]{:S(2)}) async-start(), calls=%async_computation | async-start | bytes 36175872 | tf_op jit(solution)/shard_map/psum | solution.py:251
  24.6 414.5 %copy-start.43 = (f32[10,10]{1,0:T(8,128)}, f32[10,10]{1,0:T(8,128)S(1)}, u32[]{:S(2)}) copy-start(f32[10,10]{1,0:T(8,128)S(1)} %and_convert_fusion.1) | copy-start | bytes 1204
  24.7 589.1 %copy-start.24 = (f32[20,20]{1,0:T(8,128)}, f32[20,20]{1,0:T(8,128)S(1)}, u32[]{:S(2)}) copy-start(f32[20,20]{1,0:T(8,128)S(1)} %get-tuple-element.250) | copy-start | bytes 4804
  31.3 52.0 %copy-start.5 = (f32[4,20,20,32]{3,2,1,0:T(8,128)}, f32[4,20,20,32]{3,2,1,0:T(8,128)S(1)}, u32[]{:S(2)}) copy-start(f32[4,20,20,32]{3,2,1,0:T(8,128)S(1)} %get-tuple-element.251) | copy-start | bytes 614404
  32.8 56.3 %copy-start = (f32[4,20,20,160]{3,2,1,0:T(8,128)}, f32[4,20,20,160]{3,2,1,0:T(8,128)S(1)}, u32[]{:S(2)}) copy-start(f32[4,20,20,160]{3,2,1,0:T(8,128)S(1)} %get-tuple-element.252) | copy-start | bytes 3072004
  35.0 48.3 %copy-start.180 = (f32[32]{0:T(128)S(1)}, f32[32]{0:T(128)}, u32[]{:S(2)}) copy-start(f32[32]{0:T(128)} %get-tuple-element.195) | copy-start | bytes 388
  35.0 48.3 %copy-start.183 = (f32[32]{0:T(128)S(1)}, f32[32]{0:T(128)}, u32[]{:S(2)}) copy-start(f32[32]{0:T(128)} %get-tuple-element.193) | copy-start | bytes 388
  110.0 43.7 %copy-start.205 = (f32[128]{0:T(128)S(1)}, f32[128]{0:T(128)}, u32[]{:S(2)}) copy-start(f32[128]{0:T(128)} %get-tuple-element.185) | copy-start | bytes 1540
  110.0 43.7 %copy-start.207 = (f32[128]{0:T(128)S(1)}, f32[128]{0:T(128)}, u32[]{:S(2)}) copy-start(f32[128]{0:T(128)} %get-tuple-element.182) | copy-start | bytes 1540
  111.3 43.3 %copy-start.16 = (f32[4,20,20,128]{3,2,1,0:T(8,128)}, f32[4,20,20,128]{3,2,1,0:T(8,128)S(1)}, u32[]{:S(2)}) copy-start(f32[4,20,20,128]{3,2,1,0:T(8,128)S(1)} %get-tuple-element.253) | copy-start | bytes 2457604
  365.9 15.5 %copy-start.175 = (f32[128]{0:T(128)}, f32[128]{0:T(128)S(1)}, u32[]{:S(2)}) copy-start(f32[128]{0:T(128)S(1)} %get-tuple-element.152) | copy-start | bytes 1540
  366.6 19.2 %copy-start.113 = (f32[1,256]{1,0:T(1,128)}, f32[1,256]{1,0:T(1,128)S(1)}, u32[]{:S(2)}) copy-start(f32[1,256]{1,0:T(1,128)S(1)} %get-tuple-element.217) | copy-start | bytes 3076
  369.3 11.1 %copy-start.63 = (bf16[1,2,10,10,320]{4,3,2,1,0:T(8,128)(2,1)}, bf16[1,2,10,10,320]{4,3,2,1,0:T(8,128)(2,1)S(1)}, u32[]{:S(2)}) copy-start(bf16[1,2,10,10,320]{4,3,2,1,0:T(8,128)(2,1)S(1)} %fusion.156) | copy-start | bytes 384004
  369.3 11.1 %copy-start.47 = (f32[2,10,10,160]{3,2,1,0:T(8,128)S(1)}, f32[2,10,10,160]{3,2,1,0:T(8,128)}, u32[]{:S(2)}) copy-start(f32[2,10,10,160]{3,2,1,0:T(8,128)} %get-tuple-element.262) | copy-start | bytes 384004
  369.3 11.1 %copy-start.112 = (f32[1,160]{1,0:T(1,128)S(1)}, f32[1,160]{1,0:T(1,128)}, u32[]{:S(2)}) copy-start(f32[1,160]{1,0:T(1,128)} %copy-done.111) | copy-start | bytes 1924
  369.3 11.1 %copy-start.133 = (f32[160]{0:T(256)S(1)}, f32[160]{0:T(256)}, u32[]{:S(2)}) copy-start(f32[160]{0:T(256)} %copy-done.132) | copy-start | bytes 1924
  369.3 11.1 %copy-start.137 = (f32[1,160]{1,0:T(1,128)S(1)}, f32[1,160]{1,0:T(1,128)}, u32[]{:S(2)}) copy-start(f32[1,160]{1,0:T(1,128)} %get-tuple-element.188) | copy-start | bytes 1924
  369.3 11.1 %copy-start.150 = (f32[1,160]{1,0:T(1,128)S(1)}, f32[1,160]{1,0:T(1,128)}, u32[]{:S(2)}) copy-start(f32[1,160]{1,0:T(1,128)} %get-tuple-element.190) | copy-start | bytes 1924
  369.3 12.1 %copy-start.214 = (f32[2,128]{1,0:T(2,128)S(1)}, f32[2,128]{1,0:T(2,128)}, u32[]{:S(2)}) copy-start(f32[2,128]{1,0:T(2,128)} %get-tuple-element.113) | copy-start | bytes 3076
  369.3 12.1 %copy-start.57 = (f32[2,10,10,128]{3,2,1,0:T(8,128)S(1)}, f32[2,10,10,128]{3,2,1,0:T(8,128)}, u32[]{:S(2)}) copy-start(f32[2,10,10,128]{3,2,1,0:T(8,128)} %get-tuple-element.259) | copy-start | bytes 307204
  369.3 12.1 %copy-start.69 = (f32[1,2,10,10,128]{4,0,3,2,1:T(1,128)S(1)}, f32[1,2,10,10,128]{4,0,3,2,1:T(1,128)}, u32[]{:S(2)}) copy-start(f32[1,2,10,10,128]{4,0,3,2,1:T(1,128)} %copy-done.67) | copy-start | bytes 307204
  369.3 12.1 %copy-start.79 = (f32[1,2,10,10,128]{4,3,2,1,0:T(8,128)S(1)}, f32[1,2,10,10,128]{4,3,2,1,0:T(8,128)}, u32[]{:S(2)}) copy-start(f32[1,2,10,10,128]{4,3,2,1,0:T(8,128)} %get-tuple-element.164) | copy-start | bytes 307204
  369.4 12.1 %copy-start.201 = (f32[128]{0:T(128)S(1)}, f32[128]{0:T(128)}, u32[]{:S(2)}) copy-start(f32[128]{0:T(128)} %get-tuple-element.187) | copy-start | bytes 1540
  369.4 12.1 %copy-start.203 = (f32[128]{0:T(128)S(1)}, f32[128]{0:T(128)}, u32[]{:S(2)}) copy-start(f32[128]{0:T(128)} %get-tuple-element.180) | copy-start | bytes 1540
  369.4 12.1 %copy-start.212 = (f32[128]{0:T(128)S(1)}, f32[128]{0:T(128)}, u32[]{:S(2)}) copy-start(f32[128]{0:T(128)} %copy-done.211) | copy-start | bytes 1540
  369.4 12.1 %copy-start.230 = (f32[128]{0:T(128)S(1)}, f32[128]{0:T(128)}, u32[]{:S(2)}) copy-start(f32[128]{0:T(128)} %get-tuple-element.159) | copy-start | bytes 1540
  369.4 12.1 %copy-start.240 = (f32[128]{0:T(128)S(1)}, f32[128]{0:T(128)}, u32[]{:S(2)}) copy-start(f32[128]{0:T(128)} %copy-done.239) | copy-start | bytes 1540
  369.4 13.9 %copy-start.245 = (bf16[2,3,3,3,32,128]{5,4,3,2,1,0:T(8,128)(2,1)S(1)}, bf16[2,3,3,3,32,128]{5,4,3,2,1,0:T(8,128)(2,1)}, u32[]{:S(2)}) copy-start(bf16[2,3,3,3,32,128]{5,4,3,2,1,0:T(8,128)(2,1)} %param.20) | copy-start | bytes 1327108
  457.3 24.8 %copy-start.20 = (f32[1,4,20,20,128]{4,1,3,2,0:T(4,128)}, f32[1,4,20,20,128]{4,1,3,2,0:T(4,128)S(1)}, u32[]{:S(2)}) copy-start(f32[1,4,20,20,128]{4,1,3,2,0:T(4,128)S(1)} %get-tuple-element.168) | copy-start | bytes 2457604
  482.1 42.9 %copy-start.143 = (f32[1,256]{1,0:T(1,128)S(1)}, f32[1,256]{1,0:T(1,128)}, u32[]{:S(2)}) copy-start(f32[1,256]{1,0:T(1,128)} %get-tuple-element.177) | copy-start | bytes 3076
  482.1 42.9 %copy-start.170 = (f32[1,256]{1,0:T(1,128)S(1)}, f32[1,256]{1,0:T(1,128)}, u32[]{:S(2)}) copy-start(f32[1,256]{1,0:T(1,128)} %get-tuple-element.179) | copy-start | bytes 3076
  560.5 48.0 %copy-start.227 = (f32[256]{0:T(256)S(1)}, f32[256]{0:T(256)}, u32[]{:S(2)}) copy-start(f32[256]{0:T(256)} %get-tuple-element.205) | copy-start | bytes 3076
  616.0 49.9 %copy-start.8 = (f32[4,20,20,32]{3,2,1,0:T(8,128)S(1)}, f32[4,20,20,32]{3,2,1,0:T(8,128)}, u32[]{:S(2)}) copy-start(f32[4,20,20,32]{3,2,1,0:T(8,128)} %copy-done.5) | copy-start | bytes 614404
  616.0 49.9 %copy-start.25 = (f32[20,20]{1,0:T(8,128)S(1)}, f32[20,20]{1,0:T(8,128)}, u32[]{:S(2)}) copy-start(f32[20,20]{1,0:T(8,128)} %copy-done.24) | copy-start | bytes 4804
  616.0 49.9 %copy-start.149 = (f32[32]{0:T(128)S(1)}, f32[32]{0:T(128)}, u32[]{:S(2)}) copy-start(f32[32]{0:T(128)} %copy-done.146) | copy-start | bytes 388
  616.0 49.9 %copy-start.174 = (f32[32]{0:T(128)S(1)}, f32[32]{0:T(128)}, u32[]{:S(2)}) copy-start(f32[32]{0:T(128)} %copy-done.171) | copy-start | bytes 388
  616.0 49.9 %copy-start.228 = (f32[32]{0:T(128)S(1)}, f32[32]{0:T(128)}, u32[]{:S(2)}) copy-start(f32[32]{0:T(128)} %get-tuple-element.131) | copy-start | bytes 388
  616.0 49.9 %copy-start.233 = (f32[32]{0:T(128)S(1)}, f32[32]{0:T(128)}, u32[]{:S(2)}) copy-start(f32[32]{0:T(128)} %get-tuple-element.237) | copy-start | bytes 388
  616.1 49.9 %copy-start.234 = (f32[32]{0:T(128)S(1)}, f32[32]{0:T(128)}, u32[]{:S(2)}) copy-start(f32[32]{0:T(128)} %get-tuple-element.238) | copy-start | bytes 388
  670.4 10.1 copy-start.18
  670.4 10.1 copy-start.31
  670.4 10.1 copy-start.188
  670.4 10.1 copy-start.192
  670.5 10.4 %copy-start.39 = (bf16[4,20,20,832]{3,2,1,0:T(8,128)(2,1)S(1)}, bf16[4,20,20,832]{3,2,1,0:T(8,128)(2,1)}, u32[]{:S(2)}) copy-start(bf16[4,20,20,832]{3,2,1,0:T(8,128)(2,1)} %fusion.11) | copy-start | bytes 7987204
  685.1 11.0 %copy-start.106 = (f32[1,832,32]{1,2,0:T(8,128)S(1)}, f32[1,832,32]{1,2,0:T(8,128)}, u32[]{:S(2)}) copy-start(f32[1,832,32]{1,2,0:T(8,128)} %convolution_bitcast_fusion.9) | copy-start | bytes 319492
  685.2 11.7 %copy-start.90 = (f32[1,3,3,3,32,128]{5,4,3,2,1,0:T(8,128)S(1)}, f32[1,3,3,3,32,128]{5,4,3,2,1,0:T(8,128)}, u32[]{:S(2)}) copy-start(f32[1,3,3,3,32,128]{5,4,3,2,1,0:T(8,128)} %convolution_bitcast_fusion.6) | copy-start | bytes 1327108
  1001.8 10.7 %copy-start.105 = (f32[2,832,32]{1,2,0:T(8,128)S(1)}, f32[2,832,32]{1,2,0:T(8,128)}, u32[]{:S(2)}) copy-start(f32[2,832,32]{1,2,0:T(8,128)} %get-tuple-element.270) | copy-start | bytes 638980
  1001.8 11.4 %copy-start.70 = (f32[2,3,3,3,32,128]{5,4,3,2,1,0:T(8,128)S(1)}, f32[2,3,3,3,32,128]{5,4,3,2,1,0:T(8,128)}, u32[]{:S(2)}) copy-start(f32[2,3,3,3,32,128]{5,4,3,2,1,0:T(8,128)} %get-tuple-element.271) | copy-start | bytes 2654212
  (209 other events, 646.5 us)
Sparse Core Ops, SparseCore 0:
  699.1 298.8 all-reduce.22
